TPU v7x, 128 devices: a whole 4x4x4 slice. The times are simulated.
128 devices in a mesh: seq: 8 (over z_lo, x), batch: 4 (over y), shard: 4 (over z_hi, core).
Axes of the slice: x: 4, y: 4, z: 4 (z_hi: 2, z_lo: 2; z = z_hi * 2 + z_lo), core: 2. Of those that a mesh axis runs over, the one named last changes fastest.
Arguments:
- tokens: bfloat16 [16, 3072, 640], P(('batch', 'shard'), 'seq'), may hold values from -6 to 6
- cotangent: bfloat16 [16, 3072, 640], P(('batch', 'shard'), 'seq'), may hold values from -15 to 15
- positions: int32 [16, 3072], P(('batch', 'shard'), 'seq'), may hold values from 0 to 2688, as said below
- weight_qkv: float32 [640, 1536], P(('batch', 'shard')), may hold values from -0.25 to 0.25
- weight_out: float32 [1024, 640], P(('batch', 'shard')), may hold values from -0.1875 to 0.1875
- weight_up: float32 [640, 4096], P(('batch', 'shard')), may hold values from -0.25 to 0.25
- weight_down: float32 [2048, 640], P(('batch', 'shard')), may hold values from -0.125 to 0.125
- norm_gains: float32 [3072], P(('batch', 'shard')), may hold values from -0.15 to 0.15
- first_qkv: float32 [640, 1536], P(('batch', 'shard')), may hold values from -40 to 40
- first_out: float32 [1024, 640], P(('batch', 'shard')), may hold values from -128 to 128
- first_up: float32 [640, 4096], P(('batch', 'shard')), may hold values from -80 to 80
- first_down: float32 [2048, 640], P(('batch', 'shard')), may hold values from -128 to 128
- first_gains: float32 [3072], P(('batch', 'shard')), may hold values from -128 to 128
- second_qkv: float32 [640, 1536], P(('batch', 'shard')), may hold values from 232.98048 to 928.9728
- second_out: float32 [1024, 640], P(('batch', 'shard')), may hold values from 2585.3953 to 10321.92
- second_up: float32 [640, 4096], P(('batch', 'shard')), may hold values from 648.8064 to 2585.3953
- second_down: float32 [2048, 640], P(('batch', 'shard')), may hold values from 2585.3953 to 10321.92
- second_gains: float32 [3072], P(('batch', 'shard')), may hold values from 2585.3953 to 10321.92
Outputs:
- output_tokens: bfloat16 [16, 3072, 640], P(('batch', 'shard'), 'seq')
- grad_tokens: float32 [16, 3072, 640], P(('batch', 'shard'), 'seq')
- new_qkv: float32 [640, 1536], P(('batch', 'shard'))
- new_out: float32 [1024, 640], P(('batch', 'shard'))
- new_up: float32 [640, 4096], P(('batch', 'shard'))
- new_down: float32 [2048, 640], P(('batch', 'shard'))
- new_gains: float32 [3072], P(('batch', 'shard'))
- mean_qkv: float32 [640, 1536], P(('batch', 'shard'))
- mean_out: float32 [1024, 640], P(('batch', 'shard'))
- mean_up: float32 [640, 4096], P(('batch', 'shard'))
- mean_down: float32 [2048, 640], P(('batch', 'shard'))
- mean_gains: float32 [3072], P(('batch', 'shard'))
- square_qkv: float32 [640, 1536], P(('batch', 'shard'))
- square_out: float32 [1024, 640], P(('batch', 'shard'))
- square_up: float32 [640, 4096], P(('batch', 'shard'))
- square_down: float32 [2048, 640], P(('batch', 'shard'))
- square_gains: float32 [3072], P(('batch', 'shard'))
Inputs may be any that keep to these rules, and one draw needn't show every extreme that they name: `positions`: each row of 3072 tokens holds three documents one after another (the first and last may be empty), and a token's position counts from its document's first token; the first and last documents together hold 383 tokens, so the middle one starts within the first 384 tokens, ends within the last 384, and has 2689 tokens.
All inputs are finite; a program needn't handle non-finite values.
Results may differ from a plain program's by a relative error of at most 0.018.
Values may be sent and summed in bfloat16 or wider, within the bound.
A program may use at most 128 MiB of HBM per device.

v0:
```python
import functools

import jax
import jax.numpy as jnp
from jax import lax
from jax.sharding import PartitionSpec as P

D = 640
FF = 2048
HEADS = 4
HD = 256
WINDOW = 512
STEP = 10


NORM_EPS = 1e-06
ADAM_EPS = 1e-08
BETA_ONE = 0.9
BETA_TWO = 0.95
LEARN_RATE = 0.02
WEIGHT_DECAY = 0.1
ROPE_BASE = 10000.0
SCORE_SCALE = 0.0625


def passed_along(block, axis, distance):
    devices = range(lax.axis_size(axis))
    route = [(i - distance, i) for i in devices if i - distance in devices]
    return lax.ppermute(block, axis, route)


def rms_norm(value, gain):
    scale = lax.rsqrt(jnp.mean(value * value, axis=-1, keepdims=True) + NORM_EPS)
    return value * scale * (1.0 + gain)


def rotary(value, cosine, sine):
    half_width = value.shape[-1] // 2
    lower = value[..., :half_width]
    upper = value[..., half_width:]
    return jnp.concatenate([lower * cosine - upper * sine, upper * cosine + lower * sine], axis=-1)


def tables(places):
    freqs = ROPE_BASE ** (-(jnp.arange(HD // 2) * 2.0 / HD))
    angle = places.astype(jnp.float32)[:, None] * freqs[None, :].astype(jnp.float32)
    return (jnp.cos(angle), jnp.sin(angle))


def window_mask(query_ids, key_ids, query_starts):
    later = key_ids[None, :] >= query_starts[:, None]
    causal = key_ids[None, :] <= query_ids[:, None]
    inside = query_ids[:, None] - key_ids[None, :] < WINDOW
    return later & causal & inside


def qk_prepare(raw_query, raw_key, gain_query, gain_key, cosine, sine):
    queries = rotary(rms_norm(raw_query, gain_query), cosine[:, None, :], sine[:, None, :])
    key_rows = rotary(rms_norm(raw_key, gain_key), cosine, sine)
    return (queries, key_rows)


def geglu(gate_up):
    return jax.nn.gelu(gate_up[:, :FF], approximate=True) * gate_up[:, FF:]


def adamw(weight, gradient, moment_one, moment_two, decay_rate):
    moment_one = BETA_ONE * moment_one + (1.0 - BETA_ONE) * gradient
    moment_two = BETA_TWO * moment_two + (1.0 - BETA_TWO) * gradient * gradient
    fix_one = 1.0 - BETA_ONE**STEP
    fix_two = 1.0 - BETA_TWO**STEP
    change = (
        moment_one / fix_one / (jnp.sqrt(moment_two / fix_two) + ADAM_EPS) + decay_rate * weight
    )
    return (weight - LEARN_RATE * change, moment_one, moment_two)


def shards(
    tokens,
    cotangent,
    positions,
    weight_qkv,
    weight_out,
    weight_up,
    weight_down,
    norm_gains,
    first_qkv,
    first_out,
    first_up,
    first_down,
    first_gains,
    second_qkv,
    second_out,
    second_up,
    second_down,
    second_gains,
):
    wide_qkv, wide_out, wide_up, wide_down, wide_gains = (
        lax.all_gather(weight_qkv.astype(jnp.bfloat16), ("batch", "shard"), axis=0, tiled=True),
        lax.all_gather(weight_out.astype(jnp.bfloat16), ("batch", "shard"), axis=0, tiled=True),
        lax.all_gather(weight_up.astype(jnp.bfloat16), ("batch", "shard"), axis=0, tiled=True),
        lax.all_gather(weight_down.astype(jnp.bfloat16), ("batch", "shard"), axis=0, tiled=True),
        lax.all_gather(norm_gains.astype(jnp.bfloat16), ("batch", "shard"), axis=0, tiled=True),
    )
    gain_all = wide_gains.astype(jnp.float32)
    gain_in = gain_all[:D]
    gain_attn = gain_all[D : 2 * D]
    gain_pre = gain_all[2 * D : 3 * D]
    gain_post = gain_all[3 * D : 4 * D]
    gain_query = gain_all[4 * D : 4 * D + HD]
    gain_key = gain_all[4 * D + HD :]
    inputs = tokens[0].astype(jnp.float32)
    grad_output = cotangent[0].astype(jnp.float32)
    places = positions[0]
    row_count = inputs.shape[0]
    offset = lax.axis_index("seq") * row_count
    token_ids = offset + jnp.arange(row_count, dtype=jnp.int32)
    starts = token_ids - places
    cosine, sine = tables(places)
    width_q = HEADS * HD
    normed_in, in_pull = jax.vjp(rms_norm, inputs, gain_in)
    normed_low = normed_in.astype(jnp.bfloat16)
    projected = jnp.dot(normed_low, wide_qkv, preferred_element_type=jnp.float32)
    raw_query = projected[:, :width_q].reshape(row_count, HEADS, HD)
    raw_key = projected[:, width_q : width_q + HD]
    raw_value = projected[:, width_q + HD :]
    prepare = functools.partial(qk_prepare, cosine=cosine, sine=sine)
    (queries, key_rows), qk_pull = jax.vjp(prepare, raw_query, raw_key, gain_query, gain_key)
    query_low = queries.astype(jnp.bfloat16)
    kv_own = jnp.concatenate([key_rows, raw_value], axis=1).astype(jnp.bfloat16)
    hop_total = -(-WINDOW // row_count)
    pieces = []
    current = kv_own
    for hop_number in range(hop_total):
        current = passed_along(current, "seq", 1)
        pieces.insert(0, current)
    kv_all = jnp.concatenate(pieces + [kv_own], axis=0)
    own_first = hop_total * row_count
    key_ids = offset - own_first + jnp.arange((hop_total + 1) * row_count, dtype=jnp.int32)
    block_rows = min(row_count, 512)
    key_count = block_rows + WINDOW

    def block_scores(block_index):
        start_row = block_index * block_rows
        key_first = own_first + start_row - WINDOW
        block_kv = kv_all[key_first : key_first + key_count]
        visible = window_mask(token_ids, key_ids[key_first : key_first + key_count], starts)
        scores = (
            jnp.einsum(
                "qhd,kd->hqk", query_low, block_kv[:, :HD], preferred_element_type=jnp.float32
            )
            * SCORE_SCALE
        )
        return (jnp.where(visible[None], scores, -1e30), block_kv, query_low, key_first)

    block_index = 0
    scores, block_kv, block_query, key_first = block_scores(block_index)
    row_max = jnp.max(scores, axis=-1, keepdims=True)
    exponent = jnp.exp(scores - row_max)
    row_total = jnp.sum(exponent, axis=-1, keepdims=True)
    attention = (exponent / row_total).astype(jnp.bfloat16)
    log_totals = [row_max + jnp.log(row_total)]
    contexts = jnp.einsum(
        "hqk,kd->qhd", attention, block_kv[:, HD:], preferred_element_type=jnp.float32
    )
    context_low = contexts.reshape(row_count, width_q).astype(jnp.bfloat16)
    attn_raw = jnp.dot(context_low, wide_out, preferred_element_type=jnp.float32)
    attn_normed, attn_pull = jax.vjp(rms_norm, attn_raw, gain_attn)
    middle = inputs + attn_normed
    normed_ff, pre_pull = jax.vjp(rms_norm, middle, gain_pre)
    ff_low = normed_ff.astype(jnp.bfloat16)
    gate_up = jnp.dot(ff_low, wide_up, preferred_element_type=jnp.float32)
    hidden, glu_pull = jax.vjp(geglu, gate_up)
    hidden_low = hidden.astype(jnp.bfloat16)
    ffn_raw = jnp.dot(hidden_low, wide_down, preferred_element_type=jnp.float32)
    ffn_normed, post_pull = jax.vjp(rms_norm, ffn_raw, gain_post)
    output_tokens = (middle + ffn_normed).astype(jnp.bfloat16)[None]
    d_ffn_raw, d_gain_post = post_pull(grad_output)
    d_ffn_low = d_ffn_raw.astype(jnp.bfloat16)
    grad_down = jnp.einsum("tf,td->fd", hidden_low, d_ffn_low, preferred_element_type=jnp.float32)
    d_hidden = jnp.einsum("td,fd->tf", d_ffn_low, wide_down, preferred_element_type=jnp.float32)
    (d_gate_up,) = glu_pull(d_hidden)
    d_gate_low = d_gate_up.astype(jnp.bfloat16)
    grad_up = jnp.einsum("td,tf->df", ff_low, d_gate_low, preferred_element_type=jnp.float32)
    d_normed_ff = jnp.einsum("tf,df->td", d_gate_low, wide_up, preferred_element_type=jnp.float32)
    d_middle_norm, d_gain_pre = pre_pull(d_normed_ff)
    d_middle = grad_output + d_middle_norm
    d_attn_raw, d_gain_attn = attn_pull(d_middle)
    d_attn_low = d_attn_raw.astype(jnp.bfloat16)
    grad_out = jnp.einsum("tc,td->cd", context_low, d_attn_low, preferred_element_type=jnp.float32)
    d_context = jnp.einsum("td,cd->tc", d_attn_low, wide_out, preferred_element_type=jnp.float32)
    d_context = d_context.astype(jnp.bfloat16).reshape(row_count, HEADS, HD)
    d_kv_all = jnp.zeros(((hop_total + 1) * row_count, 2 * HD), jnp.float32)
    block_index = 0
    scores, block_kv, block_query, key_first = block_scores(block_index)
    attention = jnp.exp(scores - log_totals[block_index])
    start_row = block_index * block_rows
    d_attention = jnp.einsum(
        "qhd,kd->hqk", d_context, block_kv[:, HD:], preferred_element_type=jnp.float32
    )
    row_inner = jnp.sum(attention * d_attention, axis=-1, keepdims=True)
    d_scores = (attention * (d_attention - row_inner)).astype(jnp.bfloat16)
    d_query_parts = (
        jnp.einsum("hqk,kd->qhd", d_scores, block_kv[:, :HD], preferred_element_type=jnp.float32)
        * SCORE_SCALE
    )
    d_key_part = (
        jnp.einsum("hqk,qhd->kd", d_scores, block_query, preferred_element_type=jnp.float32)
        * SCORE_SCALE
    )
    d_value_part = jnp.einsum(
        "hqk,qhd->kd", attention.astype(jnp.bfloat16), d_context, preferred_element_type=jnp.float32
    )
    d_kv_all = d_kv_all.at[key_first : key_first + key_count].add(
        jnp.concatenate([d_key_part, d_value_part], axis=1)
    )
    d_pieces = [
        d_kv_all[piece_index * row_count : (piece_index + 1) * row_count]
        for piece_index in range(hop_total + 1)
    ]
    carried = d_pieces[0]
    for piece_index in range(1, hop_total + 1):
        carried = passed_along(carried, "seq", -1) + d_pieces[piece_index]
    d_raw_query, d_raw_key, d_gain_query, d_gain_key = qk_pull((d_query_parts, carried[:, :HD]))
    d_projected = jnp.concatenate(
        [d_raw_query.reshape(row_count, width_q), d_raw_key, carried[:, HD:]], axis=1
    ).astype(jnp.bfloat16)
    grad_qkv = jnp.einsum("td,tc->dc", normed_low, d_projected, preferred_element_type=jnp.float32)
    d_normed_in = jnp.einsum("tc,dc->td", d_projected, wide_qkv, preferred_element_type=jnp.float32)
    d_input_norm, d_gain_in = in_pull(d_normed_in)
    grad_tokens = (d_middle + d_input_norm)[None]
    grad_gains = jnp.concatenate(
        [d_gain_in, d_gain_attn, d_gain_pre, d_gain_post, d_gain_query, d_gain_key]
    )
    owned_qkv, owned_out, owned_up, owned_down, owned_gains = (
        lax.psum_scatter(grad_qkv, ("batch", "shard"), scatter_dimension=0, tiled=True),
        lax.psum_scatter(grad_out, ("batch", "shard"), scatter_dimension=0, tiled=True),
        lax.psum_scatter(grad_up, ("batch", "shard"), scatter_dimension=0, tiled=True),
        lax.psum_scatter(grad_down, ("batch", "shard"), scatter_dimension=0, tiled=True),
        lax.psum_scatter(grad_gains, ("batch", "shard"), scatter_dimension=0, tiled=True),
    )
    total_qkv, total_out, total_up, total_down, total_gains = lax.psum(
        (owned_qkv, owned_out, owned_up, owned_down, owned_gains), "seq"
    )
    new_qkv, mean_qkv, square_qkv = adamw(
        weight_qkv, total_qkv, first_qkv, second_qkv, WEIGHT_DECAY
    )
    new_out, mean_out, square_out = adamw(
        weight_out, total_out, first_out, second_out, WEIGHT_DECAY
    )
    new_up, mean_up, square_up = adamw(weight_up, total_up, first_up, second_up, WEIGHT_DECAY)
    new_down, mean_down, square_down = adamw(
        weight_down, total_down, first_down, second_down, WEIGHT_DECAY
    )
    new_gains, mean_gains, square_gains = adamw(
        norm_gains, total_gains, first_gains, second_gains, 0.0
    )
    return (
        output_tokens,
        grad_tokens,
        new_qkv,
        new_out,
        new_up,
        new_down,
        new_gains,
        mean_qkv,
        mean_out,
        mean_up,
        mean_down,
        mean_gains,
        square_qkv,
        square_out,
        square_up,
        square_down,
        square_gains,
    )


def solution(mesh):
    return jax.shard_map(
        shards,
        mesh=mesh,
        in_specs=(
            P(("batch", "shard"), "seq", None),
            P(("batch", "shard"), "seq", None),
            P(("batch", "shard"), "seq"),
            P(("batch", "shard"), None),
            P(("batch", "shard"), None),
            P(("batch", "shard"), None),
            P(("batch", "shard"), None),
            P(("batch", "shard")),
            P(("batch", "shard"), None),
            P(("batch", "shard"), None),
            P(("batch", "shard"), None),
            P(("batch", "shard"), None),
            P(("batch", "shard")),
            P(("batch", "shard"), None),
            P(("batch", "shard"), None),
            P(("batch", "shard"), None),
            P(("batch", "shard"), None),
            P(("batch", "shard")),
        ),
        out_specs=(
            P(("batch", "shard"), "seq", None),
            P(("batch", "shard"), "seq", None),
            P(("batch", "shard"), None),
            P(("batch", "shard"), None),
            P(("batch", "shard"), None),
            P(("batch", "shard"), None),
            P(("batch", "shard")),
            P(("batch", "shard"), None),
            P(("batch", "shard"), None),
            P(("batch", "shard"), None),
            P(("batch", "shard"), None),
            P(("batch", "shard")),
            P(("batch", "shard"), None),
            P(("batch", "shard"), None),
            P(("batch", "shard"), None),
            P(("batch", "shard"), None),
            P(("batch", "shard")),
        ),
        check_vma=False,
    )
```

profile of v0, /device:TPU:0, one launch (start us, length us, event | category | flops | bytes accessed | tf_op | source)
XLA Modules:
  0.0 734.1 jit_solution(1653474107867936865)
XLA Ops:
  15.9 39.6 %all-reduce.7 = bf16[3072]{0:T(1024)(128)(2,1)S(1)} all-reduce(bf16[3072]{0:T(1024)(128)(2,1)S(1)} %dynamic-update-slice.3), channel_id=1, replica_groups=mesh['seq'=8,'batch'=4,'shard'=4] {'batch','shard'}, use_global_device_ids=true, to_apply=%add.7 | all-reduce | flops 3072 | bytes 12288
  58.3 3.4 all-gather.5.cloned.1.call-done
  71.6 4.1 collective-permute-start
  78.0 6.1 collective-permute-done
  84.1 4.4 collective-permute-start.1
  89.8 6.9 collective-permute-done.1
  104.3 9.5 %all-gather.7.cloned.1.call-done = bf16[1024,640]{1,0:T(8,128)(2,1)} async-done(((bf16[64,640]{1,0:T(8,128)(2,1)}), bf16[1024,640]{1,0:T(8,128)(2,1)}) %all-gather.7.cloned.1.call-update) | async-done | bytes 1310736 | tf_op jit(solution)/shard_map/all_gather | solution.py:100
  118.5 56.5 %all-gather.9.cloned.1.call-done = bf16[640,4096]{1,0:T(8,128)(2,1)} async-done(((bf16[40,4096]{1,0:T(8,128)(2,1)}), bf16[640,4096]{1,0:T(8,128)(2,1)}) %all-gather.9.cloned.1.call-update) | async-done | bytes 5242896 | tf_op jit(solution)/shard_map/all_gather | solution.py:101
  175.0 4.8 fusion.86
  184.6 42.3 %all-gather.11.cloned.1.call-done = bf16[2048,640]{1,0:T(8,128)(2,1)} async-done(((bf16[128,640]{1,0:T(8,128)(2,1)}), bf16[2048,640]{1,0:T(8,128)(2,1)}) %all-gather.11.cloned.1.call-update) | async-done | bytes 2621456 | tf_op jit(solution)/shard_map/all_gather | solution.py:102
  226.9 3.8 multiply_reduce_fusion.6
  232.8 3.9 fusion.28
  249.3 3.8 fusion.20
  253.2 4.0 fusion
  263.2 18.1 %collective-permute-done.2 = f32[384,512]{1,0:T(8,128)S(1)} collective-permute-done((f32[384,512]{1,0:T(8,128)S(1)}, f32[384,512]{1,0:T(8,128)S(1)}, u32[]{:S(2)}, u32[]{:S(2)}) %collective-permute-start.2) | collective-permute-done | bytes 786464 | tf_op jit(solution)/shard_map/ppermute | solution.py:29
  288.0 15.6 %collective-permute-done.3 = f32[384,512]{1,0:T(8,128)} collective-permute-done((f32[384,512]{1,0:T(8,128)}, f32[384,512]{1,0:T(8,128)}, u32[]{:S(2)}, u32[]{:S(2)}) %collective-permute-start.3) | collective-permute-done | bytes 786464 | tf_op jit(solution)/shard_map/ppermute | solution.py:29
  315.3 5.5 fusion.99
  321.5 9.9 %fusion.49 = f32[640,4096]{1,0:T(8,128)} fusion(f32[384,2048]{1,0:T(8,128)} %copy-done.14, f32[384,2048]{1,0:T(8,128)} %copy-done.13, f32[384,640]{1,0:T(8,128)S(1)} %get-tuple-element.62, f32[640]{0:T(1024)S(1)} %copy-done.38, f32[384]{0:T(512)S(1)} %copy-done.54), kind=kOutput, calls=%fused_computation.110 | convolution fusion | flops 2017148928 | bytes 17764352 | tf_op jit(solution)/shard_map/td,tf->df/dot_general | solution.py:184
  332.5 3.6 fusion.30
  337.0 82.2 %reduce-scatter.5.cloned.1.call-done = f32[40,1536]{1,0:T(8,128)} async-done(((f32[640,1536]{1,0:T(8,128)}), f32[40,1536]{1,0:T(8,128)}) %reduce-scatter.5.cloned.1.call-update) | async-done | bytes 245776 | tf_op jit(solution)/shard_map/reduce_scatter | solution.py:236
  419.2 88.1 %reduce-scatter.11.cloned.1.call-done = f32[128,640]{1,0:T(8,128)} async-done(((f32[2048,640]{1,0:T(8,128)}), f32[128,640]{1,0:T(8,128)}) %reduce-scatter.11.cloned.1.call-update) | async-done | bytes 327696 | tf_op jit(solution)/shard_map/reduce_scatter | solution.py:239
  507.3 115.9 %reduce-scatter.9.cloned.1.call-done = f32[40,4096]{1,0:T(8,128)} async-done(((f32[640,4096]{1,0:T(8,128)}), f32[40,4096]{1,0:T(8,128)}) %reduce-scatter.9.cloned.1.call-update) | async-done | bytes 655376 | tf_op jit(solution)/shard_map/reduce_scatter | solution.py:238
  631.1 65.5 %all-reduce.8 = f32[3072]{0:T(1024)S(1)} all-reduce(f32[3072]{0:T(1024)} %constant_dynamic-update-slice_fusion), channel_id=6, replica_groups=mesh['seq'=8,'batch'=4,'shard'=4] {'batch','shard'}, use_global_device_ids=true, to_apply=%region_29.30.clone | all-reduce | flops 3072 | bytes 24576
  696.7 19.4 %psum.39 = f32[192]{0:T(256)S(1)} all-reduce(f32[192]{0:T(256)S(1)} %dynamic-slice.9), channel_id=1, replica_groups=mesh['seq'=8,'batch'=4,'shard'=4] {'seq'}, use_global_device_ids=true, to_apply=%region_30.31 | all-reduce | flops 192 | bytes 1536 | tf_op jit(solution)/shard_map/psum | solution.py:242
  (307 shorter events, 100.3 us)
Async XLA Ops:
  7.2 49.5 %copy-start.5 = (bf16[1,384,640]{2,1,0:T(8,128)(2,1)S(1)}, bf16[1,384,640]{2,1,0:T(8,128)(2,1)}, u32[]{:S(2)}) copy-start(bf16[1,384,640]{2,1,0:T(8,128)(2,1)} %param.20) | copy-start | bytes 1474564
  7.2 49.8 %copy-start.90 = (s32[1,384]{1,0:T(1,128)S(1)}, s32[1,384]{1,0:T(1,128)}, u32[]{:S(2)}) copy-start(s32[1,384]{1,0:T(1,128)} %param.22) | copy-start | bytes 4612
  7.2 54.4 %all-gather.5.cloned.1.call-start = ((), (), s32[]{:S(2)}) async-start(), calls=%async_computation.4 | async-start | bytes 2088960 | tf_op jit(solution)/shard_map/all_gather | solution.py:99
  9.0 104.9 %all-gather.7.cloned.1.call-start = ((), (), s32[]{:S(2)}) async-start(), calls=%async_computation.5 | async-start | bytes 1392640 | tf_op jit(solution)/shard_map/all_gather | solution.py:100
  10.6 164.4 %all-gather.9.cloned.1.call-start = ((), (), s32[]{:S(2)}) async-start(), calls=%async_computation.6 | async-start | bytes 5570560 | tf_op jit(solution)/shard_map/all_gather | solution.py:101
  12.5 214.4 %all-gather.11.cloned.1.call-start = ((), (), s32[]{:S(2)}) async-start(), calls=%async_computation.7 | async-start | bytes 2785280 | tf_op jit(solution)/shard_map/all_gather | solution.py:102
  14.3 322.8 %reduce-scatter.7.cloned.1.call-start = ((), (), s32[]{:S(2)}) async-start(), calls=%async_computation.9 | async-start | bytes 2785280 | tf_op jit(solution)/shard_map/reduce_scatter | solution.py:237
  56.2 60.7 %copy-start.58 = (f32[640]{0:T(1024)}, f32[640]{0:T(1024)S(1)}, u32[]{:S(2)}) copy-start(f32[640]{0:T(1024)S(1)} %get-tuple-element.77) | copy-start | bytes 7684
  56.2 183.9 %copy-start.37 = (f32[640]{0:T(1024)}, f32[640]{0:T(1024)S(1)}, u32[]{:S(2)}) copy-start(f32[640]{0:T(1024)S(1)} %get-tuple-element.76) | copy-start | bytes 7684
  71.6 12.5 %collective-permute-start = (bf16[384,512]{1,0:T(8,128)(2,1)}, bf16[384,512]{1,0:T(8,128)(2,1)}, u32[]{:S(2)}, u32[]{:S(2)}) collective-permute-start(bf16[384,512]{1,0:T(8,128)(2,1)} %pad_maximum_fusion.10), channel_id=1, source_target_pairs={{0,16},{16,32},{32,48},{48,64},{64,80},{80,96},{96,112},{1,17},{17... | collective-permute-start | bytes 1179656 | tf_op jit(solution)/shard_map/ppermute | solution.py:29
  84.1 12.7 %collective-permute-start.1 = (bf16[384,512]{1,0:T(8,128)(2,1)}, bf16[384,512]{1,0:T(8,128)(2,1)S(1)}, u32[]{:S(2)}, u32[]{:S(2)}) collective-permute-start(bf16[384,512]{1,0:T(8,128)(2,1)} %collective-permute-done), channel_id=1, source_target_pairs={{0,16},{16,32},{32,48},{48,64},{64,80},{80,96},{96,112},{1,17},{17... | collective-permute-start | bytes 1179656 | tf_op jit(solution)/shard_map/ppermute | solution.py:29
  117.9 122.2 %copy-start.53 = (f32[384]{0:T(512)}, f32[384]{0:T(512)S(1)}, u32[]{:S(2)}) copy-start(f32[384]{0:T(512)S(1)} %fusion.76) | copy-start | bytes 4612
  248.9 170.3 %reduce-scatter.5.cloned.1.call-start = ((), (), s32[]{:S(2)}) async-start(), calls=%async_computation.8 | async-start | bytes 4177920 | tf_op jit(solution)/shard_map/reduce_scatter | solution.py:236
  259.6 21.7 %collective-permute-start.2 = (f32[384,512]{1,0:T(8,128)S(1)}, f32[384,512]{1,0:T(8,128)S(1)}, u32[]{:S(2)}, u32[]{:S(2)}) collective-permute-start(f32[384,512]{1,0:T(8,128)S(1)} %pad_slice_fusion.4), channel_id=1, source_target_pairs={{16,0},{32,16},{48,32},{64,48},{80,64},{96,80},{112,96},{17,1},{33... | collective-permute-start | bytes 2359304 | tf_op jit(solution)/shard_map/ppermute | solution.py:29
  282.3 21.3 %collective-permute-start.3 = (f32[384,512]{1,0:T(8,128)}, f32[384,512]{1,0:T(8,128)}, u32[]{:S(2)}, u32[]{:S(2)}) collective-permute-start(f32[384,512]{1,0:T(8,128)} %fusion.40), channel_id=1, source_target_pairs={{16,0},{32,16},{48,32},{64,48},{80,64},{96,80},{112,96},{17,1},{33... | collective-permute-start | bytes 2359304 | tf_op jit(solution)/shard_map/ppermute | solution.py:29
  287.9 23.1 %copy-start.11 = (bf16[384,4,256]{0,2,1:T(8,128)(2,1)}, bf16[384,4,256]{0,2,1:T(8,128)(2,1)S(1)}, u32[]{:S(2)}) copy-start(bf16[384,4,256]{0,2,1:T(8,128)(2,1)S(1)} %copy.120) | copy-start | bytes 2359300
  288.0 23.1 %copy-start.7 = (bf16[1,384,640]{2,1,0:T(8,128)(2,1)S(1)}, bf16[1,384,640]{2,1,0:T(8,128)(2,1)}, u32[]{:S(2)}) copy-start(bf16[1,384,640]{2,1,0:T(8,128)(2,1)} %param.20) | copy-start | bytes 1474564
  288.0 23.1 %copy-start.56 = (f32[640]{0:T(1024)S(1)}, f32[640]{0:T(1024)}, u32[]{:S(2)}) copy-start(f32[640]{0:T(1024)} %copy-done.55) | copy-start | bytes 7684
  314.3 193.0 %reduce-scatter.11.cloned.1.call-start = ((), (), s32[]{:S(2)}) async-start(), calls=%async_computation.11 | async-start | bytes 5570560 | tf_op jit(solution)/shard_map/reduce_scatter | solution.py:239
  320.8 302.4 %reduce-scatter.9.cloned.1.call-start = ((), (), s32[]{:S(2)}) async-start(), calls=%async_computation.10 | async-start | bytes 11141120 | tf_op jit(solution)/shard_map/reduce_scatter | solution.py:238
  331.4 388.7 %all-reduce.12.cloned.1.call-start = ((), (), s32[]{:S(2)}) async-start(), calls=%async_computation.12 | async-start | bytes 2785280 | tf_op jit(solution)/shard_map/psum | solution.py:242
  332.5 385.6 %copy-start.4 = (f32[384,640]{1,0:T(8,128)S(1)}, f32[384,640]{1,0:T(8,128)}, u32[]{:S(2)}) copy-start(f32[384,640]{1,0:T(8,128)} %copy-done.3) | copy-start | bytes 2949124
  336.1 383.9 %copy-start.28 = (f32[40,1536]{1,0:T(8,128)S(1)}, f32[40,1536]{1,0:T(8,128)}, u32[]{:S(2)}) copy-start(f32[40,1536]{1,0:T(8,128)} %param.23) | copy-start | bytes 737284
  623.3 99.1 %copy-start.42 = (f32[64,640]{1,0:T(8,128)S(1)}, f32[64,640]{1,0:T(8,128)}, u32[]{:S(2)}) copy-start(f32[64,640]{1,0:T(8,128)} %param.24) | copy-start | bytes 491524
  (86 other events, 540.4 us)
Sparse Core Ops, SparseCore 0:
  11.0 50.5 all-gather.4
  64.6 49.1 all-gather.6
  116.8 58.1 all-gather.8
  177.8 49.0 all-gather.10
  249.0 87.9 reduce-scatter.6
  341.5 77.6 reduce-scatter.4
  423.8 83.4 reduce-scatter.10
  512.3 110.8 reduce-scatter.8
  626.0 77.9 all-reduce.11
where the time goes:
time: 743 us; the launch traced here: 734 us
  waiting for transfers between devices  446 us (60%)
  blocking collectives  124 us (17%)
  matrix products  63.8 us (9%)
  other arithmetic  45.1 us (6%)
  local copies, waits for them, and re-layouts  26 us (3%)
  between operations  17 us (2%)
  starting transfers between devices  12.1 us (2%)
    reduce_scatter x1, waiting for transfers between devices, shards(): lax.psum_scatter(grad_up, ('batch', 'shard'), scatter_dimension=0, tiled=...  116 us
    unnamed x2, blocking collectives  105 us
    reduce_scatter x1, waiting for transfers between devices, shards(): lax.psum_scatter(grad_down, ('batch', 'shard'), scatter_dimension=0, tile...  88.1 us
    reduce_scatter x1, waiting for transfers between devices, shards(): lax.psum_scatter(grad_qkv, ('batch', 'shard'), scatter_dimension=0, tiled...  82.2 us
    all_gather x1, waiting for transfers between devices, shards(): lax.all_gather(weight_up.astype(jnp.bfloat16), ('batch', 'shard'), axis=0...  56.5 us
    ppermute x4, waiting for transfers between devices, passed_along(): return lax.ppermute(block, axis, route)  46.7 us
    all_gather x1, waiting for transfers between devices, shards(): lax.all_gather(weight_down.astype(jnp.bfloat16), ('batch', 'shard'), axis...  42.3 us
    psum x1, blocking collectives, shards(): lax.psum((owned_qkv, owned_out, owned_up, owned_down, owned_gains), 'seq')  19.4 us
  transfers between devices with their start and end apart: 13, of which 12 were waited for; matrix products, arithmetic and copies ran while one was open for 13% of the time, Pallas kernels for 0%

commit v1 on v0

v1 whole, which is shorter than its diff:
```python
import jax
import numpy as np
import jax.numpy as jnp
from jax import lax
from jax.experimental import pallas as pl
from jax.experimental.pallas import tpu as pltpu
from jax.sharding import PartitionSpec as P

D = 640
FF = 2048
HEADS = 4
HD = 256
WINDOW = 512
STEP = 10


NORM_EPS = 1e-06
ADAM_EPS = 1e-08
BETA_ONE = 0.9
BETA_TWO = 0.95
LEARN_RATE = 0.02
WEIGHT_DECAY = 0.1
ROPE_BASE = 10000.0
SCORE_SCALE = 0.0625
MESH = pl.DeviceIdType.MESH


def tables():
    return np.float32(ROPE_BASE ** (-(np.arange(HD // 2) * 2.0 / HD)))[None]


def adamw(weight, gradient, moment_one, moment_two, decay_rate):
    moment_one = BETA_ONE * moment_one + (1.0 - BETA_ONE) * gradient
    moment_two = BETA_TWO * moment_two + (1.0 - BETA_TWO) * gradient * gradient
    fix_one = 1.0 - BETA_ONE**STEP
    fix_two = 1.0 - BETA_TWO**STEP
    change = (
        moment_one / fix_one / (jnp.sqrt(moment_two / fix_two) + ADAM_EPS) + decay_rate * weight
    )
    return (weight - LEARN_RATE * change, moment_one, moment_two)


class Place:
    def __init__(self):
        seq = lax.axis_index("seq")
        shard = lax.axis_index("shard")
        self.x = lax.rem(seq, 4)
        self.zl = seq // 4
        self.y = lax.axis_index("batch")
        self.zh = shard // 2
        self.c = lax.rem(shard, 2)
        self.xp, self.xm, self.x2 = (lax.rem(self.x + k, 4) for k in (1, 3, 2))
        self.yp, self.ym, self.y2 = (lax.rem(self.y + k, 4) for k in (1, 3, 2))
        self.sib = self.at()
        self.sib["shard"] = self.zh * 2 + 1 - self.c
        self.to_xp, self.to_xm = self.at(x=self.xp), self.at(x=self.xm)
        self.to_yp, self.to_ym = self.at(y=self.yp), self.at(y=self.ym)
        self.to_zf = self.at(zl=1 - self.zl)
        self.to_zq = self.at(zl=1 - self.zl, zh=1 - self.zh)
        self.to_x2, self.to_y2 = self.at(x=self.x2), self.at(y=self.y2)
        self.to_z2 = self.at(zh=1 - self.zh)
        self.sib_zf = self.at(zl=1 - self.zl)
        self.sib_zf["shard"] = self.sib["shard"]

        for name, step in (("next", 1), ("next2", 2), ("prev", 7), ("prev2", 6)):
            there = self.at()
            there["seq"] = lax.rem(seq + step, 8)
            setattr(self, "to_" + name, there)

    def at(self, x=None, y=None, zl=None, zh=None):
        x = self.x if x is None else x
        y = self.y if y is None else y
        zl = self.zl if zl is None else zl
        zh = self.zh if zh is None else zh
        return {"seq": zl * 4 + x, "batch": y, "shard": zh * 2 + self.c}

    def neighbours(self):
        return (self.sib, self.to_xp, self.to_xm, self.to_yp, self.to_ym, self.to_zf, self.to_zq) + (
            self.to_next, self.to_next2, self.to_prev, self.to_prev2,
            self.to_x2, self.to_y2, self.to_z2, self.sib_zf,
        )


def greet(place):
    barrier = pltpu.get_barrier_semaphore()
    near = place.neighbours()
    for device in near:
        pl.semaphore_signal(barrier, inc=1, device_id=device, device_id_type=MESH)
    pl.semaphore_wait(barrier, len(near))


class Wire:
    def __init__(self, send_sems, recv_sems):
        self.send_sems, self.recv_sems, self.copies = send_sems, recv_sems, []

    def send(self, src, dst, device):
        number = len(self.copies)
        copy = pltpu.make_async_remote_copy(
            src_ref=src,
            dst_ref=dst,
            send_sem=self.send_sems.at[number],
            recv_sem=self.recv_sems.at[number],
            device_id=device,
            device_id_type=MESH,
        )
        copy.start()
        self.copies.append(copy)
        return copy

    def same(self, ref, device):
        return self.send(ref, ref, device)

    def drain(self):
        for copy in self.copies:
            copy.wait_send()


def cols(start, size):
    return pl.ds(pl.multiple_of(start, 128), size)


def rows(start, size, unit=16):
    return pl.ds(pl.multiple_of(start, unit), size)


COPIES = 192


def dot(left, right):
    return jnp.dot(left, right, preferred_element_type=jnp.float32)


def dot_nt(left, right):
    return lax.dot_general(left, right, (((1,), (1,)), ((), ())), preferred_element_type=jnp.float32)


def dot_tn(left, right):
    return lax.dot_general(left, right, (((0,), (0,)), ((), ())), preferred_element_type=jnp.float32)


def scale_of(value):
    return lax.rsqrt(jnp.mean(value * value, axis=-1, keepdims=True) + NORM_EPS)


def norm_back(grad, value, scale, gain):
    spread = gain * grad
    inner = jnp.mean(spread * value, axis=-1, keepdims=True)
    d_value = scale * spread - value * (scale * scale * scale * inner)
    d_gain = jnp.sum(grad * (value * scale), axis=0, keepdims=True)
    return d_value, d_gain


def turn(value, cosine, sine):
    lower, upper = value[:, :128], value[:, 128:]
    return jnp.concatenate([lower * cosine - upper * sine, upper * cosine + lower * sine], axis=1)


def turn_back(value, cosine, sine):
    lower, upper = value[:, :128], value[:, 128:]
    return jnp.concatenate([lower * cosine + upper * sine, upper * cosine - lower * sine], axis=1)


def gelu_parts(gate):
    root = 0.7978845608028654
    inner = jnp.tanh(root * (gate + 0.044715 * gate * gate * gate))
    half = 0.5 * (1.0 + inner)
    slope = half + 0.5 * gate * (1.0 - inner * inner) * (root * (1.0 + 3 * 0.044715 * gate * gate))
    return gate * half, slope


def low_add(*terms):
    total = terms[0].astype(jnp.float32)
    for term in terms[1:]:
        total = total + term.astype(jnp.float32)
    return total


def layer_kernel(
    tok_hbm, cot_hbm, place_ref, freq_ref, qkv_hbm, out_hbm, up_hbm, down_hbm, gain_ref,
    y_ref, dx_ref, rq, rk, ro, ru, rd, tg,
    tok_ref, cot_ref, place_col, cos_ref, sin_ref, k_in, q_in, u_in, o_in, d_in, in_sems,
    q_all, k_all, o_all, u_all, d_all, q_near, k_near, u_near, gn_c, gn_z, gn_y, gain_all,
    nin, proj, qkv_scale, qs, kv, probs, ctx, raw, mid, ffl, act, hid_x, gc_query,
    df, dg_x, d_ctx, d_kv, kv_out, kv_in1, kv_in2, fft,
    go, co, hu, hq, hk, ho, hd,
    ux1, ux2, su_, uy1, uy2, tu, uz1,
    qy1, qy2, tq, qz1, qx,
    ky1, ky2, tk, kz1, kx,
    oy1, oy2, to, oz1, ox,
    dz1, dz2, sd_, dy1, dy2, dxx,
    gc, gz, gy, gx,
    send_sems, recv_sems,
):
    low, f32 = jnp.bfloat16, jnp.float32
    p = Place()
    x, y, zl, zh, c = p.x, p.y, p.zl, p.zh, p.c
    zo, lo = 1 - zh, 1 - zl
    z, z2 = zh * 2 + zl, zo * 2 + zl
    zf, zq = zh * 2 + lo, zo * 2 + lo
    slot_one, slot_two = 2 * c, 2 - c
    dq_x, dk_x = act.at[:, :, 0:512], act.at[:, :, 512:768]

    def u_part(ax):
        return cols(c * 2048 + 512 * ax, 512)

    q_half, k_half = cols(c * 512, 512), cols(c * 256, 256)
    fetches = []
    for src, dst in (
        (qkv_hbm.at[:, cols(1024 + c * 256, 256)], k_in), (qkv_hbm.at[:, q_half], q_in),
        (up_hbm.at[:, u_part(x)], u_in), (out_hbm, o_in),
        (down_hbm, d_in), (tok_hbm, tok_ref), (cot_hbm, cot_ref),
    ):
        fetch = pltpu.make_async_copy(src, dst, in_sems.at[len(fetches)])
        fetch.start()
        fetches.append(fetch)
    greet(p)
    wire = Wire(send_sems, recv_sems)

    def recv(*copies):
        for copy in copies:
            copy.wait_recv()

    gn_c[0] = gain_ref[...]
    near_k = wire.send(qkv_hbm.at[:, cols(1280 - c * 256, 256)], k_near, p.sib)
    near_q = wire.send(qkv_hbm.at[:, cols((1 - c) * 512, 512)], q_near, p.sib)
    near_u = wire.send(up_hbm.at[:, cols((1 - c) * 2048 + 512 * x, 512)], u_near, p.sib)
    near_g = wire.send(gn_c.at[0], gn_c.at[1], p.sib)

    def pair(mine, other):
        first = jnp.where(c == 0, mine, other)
        second = jnp.where(c == 0, other, mine)
        return jnp.concatenate([first, second], axis=0).astype(low)

    fetches[0].wait()
    recv(near_k)
    k_all[y, zh, :, k_half] = pair(k_in[...], k_near[...])
    own_k = k_all.at[y, zh, :, k_half]
    kz = wire.same(own_k, p.to_zq)
    k1 = [wire.same(own_k, p.to_yp), wire.same(own_k, p.to_ym)]
    fetches[1].wait()
    recv(near_q)
    q_all[y, zh, :, q_half] = pair(q_in[...], q_near[...])
    own_q = q_all.at[y, zh, :, q_half]
    qz = wire.same(own_q, p.to_zq)
    q1 = [wire.same(own_q, p.to_yp), wire.same(own_q, p.to_ym)]
    fetches[2].wait()
    recv(near_u)
    u_all[y, zh, :, u_part(x)] = pair(u_in[...], u_near[...])
    own_u = u_all.at[y, zh, :, u_part(x)]
    uz = wire.same(own_u, p.to_zq)
    u1 = [wire.same(own_u, p.to_yp), wire.same(own_u, p.to_ym)]
    recv(near_g)
    gn_z[0] = gn_c[0] + gn_c[1]
    gzc = wire.send(gn_z.at[0], gn_z.at[1], p.to_zq)
    for fetch in fetches[3:]:
        fetch.wait()
    o_all[y, zh, c] = o_in[...].astype(low)
    d_all[y, zh, c] = d_in[...].astype(low)
    own_o, own_d = o_all.at[y, zh, c], d_all.at[y, zh, c]
    recv(kz)
    k2 = [wire.same(k_all.at[y, zo, :, k_half], to_) for to_ in (p.to_yp, p.to_ym)]
    recv(qz)
    q2 = [wire.same(q_all.at[y, zo, :, q_half], to_) for to_ in (p.to_yp, p.to_ym)]
    recv(uz)
    u2 = [wire.same(u_all.at[y, zo, :, u_part(x)], to_) for to_ in (p.to_yp, p.to_ym)]

    def round_x(k):
        piece = u_all.at[k, :, :, u_part(x)]
        return [wire.same(piece, p.to_xp), wire.same(piece, p.to_xm)]

    u4 = [round_x(y)]
    recv(gzc)
    gn_y[y] = gn_z[0] + gn_z[1]
    g2 = [wire.same(gn_y.at[y], to_) for to_ in (p.to_yp, p.to_ym, p.to_y2)]

    inputs = tok_ref[...].astype(f32)
    raw[...] = inputs * scale_of(inputs)
    for r in range(3):
        here = slice(128 * r, 128 * (r + 1))
        place = jnp.broadcast_to(place_ref[r : r + 1].astype(f32), (128, 128)).T
        place_col[here] = place
        angle = place * freq_ref[...]
        cos_ref[here] = jnp.cos(angle)
        sin_ref[here] = jnp.sin(angle)

    recv(k1[0])
    k3a = wire.same(k_all.at[p.ym, zh, :, k_half], p.to_yp)
    recv(k2[1])
    k3b = wire.same(k_all.at[p.yp, zo, :, k_half], p.to_ym)
    recv(k1[1], k2[0])
    sib_k = [wire.same(k_all.at[k, :, :, k_half], p.sib) for k in (y, p.ym, p.yp)]
    recv(q1[0])
    q3a = wire.same(q_all.at[p.ym, zh, :, q_half], p.to_yp)
    recv(q2[1])
    q3b = wire.same(q_all.at[p.yp, zo, :, q_half], p.to_ym)
    recv(u1[0])
    u3a = wire.same(u_all.at[p.ym, zh, :, u_part(x)], p.to_yp)
    recv(u2[1])
    u3b = wire.same(u_all.at[p.yp, zo, :, u_part(x)], p.to_ym)
    recv(k3a, k3b)
    sib_k.append(wire.same(k_all.at[p.y2, :, :, k_half], p.sib))
    recv(q1[1], q2[0])
    sib_q = [wire.same(q_all.at[k, :, :, q_half], p.sib) for k in (y, p.ym, p.yp)]
    recv(u1[1], u2[0])
    u4 += [round_x(p.ym), round_x(p.yp)]
    recv(*g2)
    gain_all[...] = 1.0 + ((gn_y[0] + gn_y[1]) + (gn_y[2] + gn_y[3]))
    oz = wire.same(own_o, p.to_zq)
    o1 = [wire.same(own_o, p.to_yp), wire.same(own_o, p.to_ym)]

    def gain_row(first, count):
        return jnp.concatenate([gain_all[k : k + 1] for k in range(first, first + count)], axis=1)

    def put_gain(first, grad):
        for k in range(grad.shape[1] // 128):
            gc[1, first + k : first + k + 1] = grad[:, 128 * k : 128 * (k + 1)]

    nin[c] = (raw[...] * gain_row(0, 5)).astype(low)
    nin_c = wire.same(nin.at[c], p.sib)
    u5 = []

    def pass_x(number):
        recv(u4[number][1])
        k = (y, p.ym, p.yp, p.y2)[number]
        u5.append(wire.same(u_all.at[k, :, :, u_part(p.xp)], p.to_xm))

    recv(*sib_k)

    cosine, sine = cos_ref[...], sin_ref[...]
    kv_raw = dot(nin[c], k_all[...].reshape(D, 512))
    proj[:, 1024:1280] = kv_raw[:, :HD]
    key_scale = scale_of(kv_raw[:, :HD])
    qkv_scale[:, 4:5] = key_scale
    kv[512:896, :HD] = turn(kv_raw[:, :HD] * key_scale * gain_row(22, 2), cosine, sine).astype(low)
    kv[512:896, HD:] = kv_raw[:, HD:].astype(low)
    kv_c1 = wire.send(kv.at[512:896], kv.at[128:512], p.to_next)
    kv_c2 = wire.send(kv.at[768:896], kv.at[0:128], p.to_next2)

    recv(u3a, u3b)
    u4.append(round_x(p.y2))
    sib_u = [wire.same(u_all.at[:, :, :, u_part(x)], p.sib)]
    recv(q3a, q3b)
    sib_q.append(wire.same(q_all.at[p.y2, :, :, q_half], p.sib))
    pass_x(0)
    recv(oz)
    o2 = [wire.same(o_all.at[y, zo, c], to_) for to_ in (p.to_yp, p.to_ym)]
    d1 = [wire.same(own_d, p.to_yp), wire.same(own_d, p.to_ym)]
    recv(o1[0])
    o3a = wire.same(o_all.at[p.ym, zh, c], p.to_yp)
    pass_x(1)
    recv(o2[1])
    o3b = wire.same(o_all.at[p.yp, zo, c], p.to_ym)
    recv(o1[1], o2[0])
    sib_o = [wire.same(o_all.at[k, :, c], p.sib) for k in (y, p.ym, p.yp)]
    recv(*sib_q)

    for h in range(HEADS):
        head = dot(nin[c], q_all[:, :, :, HD * h : HD * (h + 1)].reshape(D, HD))
        proj[:, HD * h : HD * (h + 1)] = head
        head_scale = scale_of(head)
        qkv_scale[:, h : h + 1] = head_scale
        qs[h] = turn(head * head_scale * gain_row(20, 2), cosine, sine).astype(low)

    recv(*d1)
    d3 = [
        wire.same(d_all.at[p.ym, zh, c, 0:64], p.to_yp),
        wire.same(d_all.at[p.yp, zh, c, 64:128], p.to_ym),
    ]
    pass_x(2)

    recv(kv_c1, kv_c2)
    row = lax.broadcasted_iota(jnp.int32, (128, 640), 0)
    column = lax.broadcasted_iota(jnp.int32, (128, 640), 1)
    distance = (row + 512 - column).astype(f32)
    for r in range(3):
        block_q = qs[:, 128 * r : 128 * (r + 1)].reshape(512, HD)
        block_kv = kv.at[128 * r : 128 * r + 640]
        furthest = jnp.minimum(place_col[128 * r : 128 * (r + 1), 0:1], WINDOW - 1.0)
        visible = (distance >= 0) & (distance <= furthest)
        scores = dot_nt(block_q, block_kv[:, :HD]).reshape(HEADS, 128, 640) * SCORE_SCALE
        scores = jnp.where(visible[None], scores, -1e30).reshape(512, 640)
        exponent = jnp.exp(scores - jnp.max(scores, axis=-1, keepdims=True))
        share = exponent * (1.0 / jnp.sum(exponent, axis=-1, keepdims=True))
        share = share.astype(low)
        probs[r] = share
        mixed = dot(share, block_kv[:, HD:])
        for h in range(HEADS):
            ctx[128 * r : 128 * (r + 1), HD * h : HD * (h + 1)] = mixed[
                128 * h : 128 * (h + 1)
            ].astype(low)
        if r == 0:
            pass_x(3)
            recv(o3a, o3b)
            sib_o.append(wire.same(o_all.at[p.y2, :, c], p.sib))
        if r == 1:
            sib_u.append(wire.same(u_all.at[:, :, :, u_part(p.xp)], p.sib))
            recv(*d3)
            d4 = wire.same(d_all.at[rows(2 * zl, 2, 2), zh, c], p.to_zq)
            sib_d = [wire.same(d_all.at[:, zh, c], p.sib)]

    recv(*sib_o)
    attn_raw = dot(ctx[...], o_all[...].reshape(HEADS * HD, D))
    raw[...] = attn_raw
    attn_scale = scale_of(attn_raw)
    qkv_scale[:, 5 : 5 + 1] = attn_scale
    middle = tok_ref[...].astype(f32) + attn_raw * attn_scale * gain_row(5, 5)
    mid[...] = middle
    mid_scale = scale_of(middle)
    qkv_scale[:, 6 : 6 + 1] = mid_scale
    ffl[c] = (middle * mid_scale * gain_row(10, 5)).astype(low)
    ffl_c = wire.same(ffl.at[c], p.sib)

    recv(d4)
    d5 = wire.same(d_all.at[rows(2 - 2 * zl, 2, 2), zo, c], p.to_zf)
    sib_d.append(wire.same(d_all.at[rows(2 - 2 * zl, 2, 2), zo, c], p.sib))
    recv(*[piece[0] for piece in u4])
    sib_u.append(wire.same(u_all.at[:, :, :, u_part(p.xm)], p.sib))

    def act_cols(k):
        return cols(256 * lax.rem(k, 6), 256)

    def up_step(i, quarter):
        k = 2 * quarter + i
        part = cols(256 * k, 256)
        gate = dot(ffl[c], u_all[:, :, :, part].reshape(D, 256))
        up = dot(ffl[c], u_all[:, :, :, cols(FF + 256 * k, 256)].reshape(D, 256))
        value, slope = gelu_parts(gate)
        act[k // 6, :, act_cols(k)] = value.astype(low)
        act[(k + 8) // 6, :, act_cols(k + 8)] = (up * slope).astype(low)
        hidden = (value * up).astype(low)
        hu[0:384, part] = hidden
        hid_x[k, slot_one] = hidden[:, :128]
        hid_x[k, slot_two] = hidden[:, 128:]
        return quarter

    for n, quarter in enumerate((x, p.xp, p.xm, p.x2)):
        if n == 3:
            recv(d5)
            sib_d.append(wire.same(d_all.at[rows(2 * zl, 2, 2), zo, c], p.sib))
            recv(*u5)
            sib_u.append(wire.same(u_all.at[:, :, :, u_part(p.x2)], p.sib))
        recv(sib_u[n])
        lax.fori_loop(0, 2, up_step, quarter)
    hid_c = wire.send(hid_x.at[:, 2], hid_x.at[:, c], p.sib)
    recv(*sib_d)
    ffn_raw = dot(hu[0:384], d_all[...].reshape(FF, D))
    ffn_scale = scale_of(ffn_raw)
    y_ref[...] = (mid[...] + ffn_raw * ffn_scale * gain_row(15, 5)).astype(low)

    d_ffn, dg_post = norm_back(cot_ref[...].astype(f32), ffn_raw, ffn_scale, gain_row(15, 5))
    put_gain(15, dg_post)
    df[c] = d_ffn.astype(low)
    df_c = wire.same(df.at[c], p.sib)

    def hidden_back(i, quarter):
        k = 2 * quarter + i
        part = cols(256 * k, 256)
        d_hidden = dot_nt(df[c], d_all[quarter, i].reshape(256, D))
        slope = act[(k + 8) // 6, :, act_cols(k + 8)].astype(f32)
        dg_x[slot_one, :, part] = (d_hidden * slope).astype(low)
        value = act[k // 6, :, act_cols(k)].astype(f32)
        dg_x[slot_two, :, part] = (d_hidden * value).astype(low)
        return quarter

    quarters = (p.x2, p.xp, p.xm, x)
    dg_c = []
    for quarter in quarters:
        lax.fori_loop(0, 2, hidden_back, quarter)
        part = cols(512 * quarter, 512)
        dg_c.append(wire.send(dg_x.at[2, :, part], dg_x.at[c, :, part], p.sib))
    recv(ffl_c)
    fft[...] = ffl[...].reshape(768, D).T

    def up_grad(n):
        recv(dg_c[n])
        part = cols(512 * quarters[n], 512)
        block = dot(fft[...], dg_x[0:2, :, part].reshape(768, 512))
        hu[:, part] = block.astype(low)

    up_grad(0)
    u_x1 = [
        wire.send(hu.at[:, cols(512 * p.x2, 256)], ux1.at[0], p.to_xm),
        wire.send(hu.at[:, cols(512 * p.x2 + 256, 256)], ux1.at[1], p.to_xp),
    ]
    up_grad(1)
    up_grad(2)
    recv(hid_c, df_c)

    def down_grad(k, _):
        block = dot_tn(hid_x[k, 0:2].reshape(768, 128), df[...].reshape(768, D))
        hd[k // 2, lax.rem(k, 2)] = block.reshape(2, 64, D).astype(low)
        return 0

    lax.fori_loop(0, 8, down_grad, 0)
    d_z1 = [
        wire.send(hd.at[0:2, zo, zl], dz1.at[0], p.to_zq),
        wire.send(hd.at[2:4, zo, zl], dz1.at[1], p.to_zf),
    ]
    up_grad(3)
    recv(*u_x1)

    def add_ux(k, _):
        here = rows(80 * k, 80)
        one, two = cols(512 * p.xm, 256), cols(512 * p.xp + 256, 256)
        hu[here, one] = low_add(hu[here, one], ux1[0, here]).astype(low)
        hu[here, two] = low_add(hu[here, two], ux1[1, here]).astype(low)
        return 0

    lax.fori_loop(0, 8, add_ux, 0)
    u_x2 = [
        wire.send(hu.at[:, cols(512 * p.xm, 512)], ux2.at[0], p.to_xm),
        wire.send(hu.at[:, cols(512 * p.xp, 512)], ux2.at[1], p.to_xp),
    ]
    recv(*d_z1)
    hd[0:2, zh, lo] = low_add(hd[0:2, zh, lo], dz1[0]).astype(low)
    hd[2:4, zo, lo] = low_add(hd[2:4, zo, lo], dz1[1]).astype(low)
    d_z2 = [
        wire.send(hd.at[:, zh, lo], dz2.at[0], p.to_zf),
        wire.send(hd.at[:, zo, lo], dz2.at[1], p.to_zq),
    ]
    d_normed = dot_nt(dg_x[slot_one], u_all[:, :, :, :FF].reshape(D, FF)) + dot_nt(
        dg_x[slot_two], u_all[:, :, :, FF:].reshape(D, FF)
    )
    d_middle, dg_pre = norm_back(d_normed, mid[...], qkv_scale[:, 6 : 6 + 1], gain_row(10, 5))
    put_gain(10, dg_pre)
    d_middle = d_middle + cot_ref[...].astype(f32)
    dx_ref[...] = d_middle
    d_attn, dg_attn = norm_back(d_middle, raw[...], qkv_scale[:, 5 : 5 + 1], gain_row(5, 5))
    put_gain(5, dg_attn)
    d_attn = d_attn.astype(low)
    d_ctx[...] = dot_nt(d_attn, o_all[...].reshape(HEADS * HD, D)).astype(low)
    go[...] = dot_tn(ctx[...], d_attn).astype(low).reshape(4, 2, 2, 64, D)
    o_c = wire.send(go.at[:, :, 1 - c], co, p.sib)

    recv(*d_z2)
    for k in range(4):
        sd_[k] = low_add(hd[k, zh, zl], dz2[0, k], dz2[1, k]).astype(low)
    d_y1 = [
        wire.send(sd_.at[p.y2, 0:32], dy1.at[0], p.to_ym),
        wire.send(sd_.at[p.y2, 32:64], dy1.at[1], p.to_yp),
    ]

    def add_us(k, _):
        i, j = k // 2, lax.rem(k, 2)
        here, part = rows(80 * k, 80), cols(512 * x, 512)
        su_[i, j] = low_add(hu[here, part], ux2[0, here], ux2[1, here]).astype(low)
        return 0

    d_kv[...] = jnp.zeros_like(d_kv)
    gc_query[...] = jnp.zeros((1, HD), f32)
    kv_b = []
    for r in range(3):
        here = slice(128 * r, 128 * (r + 1))
        span = slice(128 * r, 128 * r + 640)
        d_mixed = jnp.concatenate(
            [d_ctx[here, HD * h : HD * (h + 1)] for h in range(HEADS)], axis=0
        )
        share = probs[r].astype(f32)
        d_share = dot_nt(d_mixed, kv[span, HD:])
        d_scores = share * (d_share - jnp.sum(share * d_share, axis=-1, keepdims=True))
        d_scores = d_scores.astype(low)
        block_q = qs[:, here].reshape(512, HD)
        d_kv[span, :HD] += dot_tn(d_scores, block_q) * SCORE_SCALE
        d_kv[span, HD:] += dot_tn(probs[r], d_mixed)
        if r == 0:
            kv_out[0:128] = d_kv[0:128].astype(low)
            kv_b.append(wire.send(kv_out.at[0:128], kv_in2, p.to_prev2))
        if r == 1:
            kv_out[128:256] = d_kv[128:256].astype(low)
            kv_b.append(wire.send(kv_out.at[128:256], kv_in1.at[0:128], p.to_prev))
        if r == 2:
            kv_out[256:512] = d_kv[256:512].astype(low)
            kv_b.append(wire.send(kv_out.at[256:512], kv_in1.at[128:384], p.to_prev))
        d_query = dot(d_scores, kv[span, :HD]) * SCORE_SCALE
        for h in range(HEADS):
            piece = turn_back(d_query[128 * h : 128 * (h + 1)], cos_ref[here], sin_ref[here])
            d_head, d_gain = norm_back(
                piece, proj[here, HD * h : HD * (h + 1)], qkv_scale[here, h : h + 1], gain_row(20, 2)
            )
            gc_query[...] += d_gain
            slot, start = (slot_one, slot_two)[h // 2], HD * (h % 2)
            dq_x[slot, here, start : start + HD] = d_head.astype(low)
        if r == 0:
            recv(o_c)
            for i in range(4):
                for j in range(2):
                    ho[i, j] = low_add(go[i, j, c], co[i, j]).astype(low)
            o_y1 = [
                wire.send(ho.at[p.y2, 0], oy1.at[0], p.to_ym),
                wire.send(ho.at[p.y2, 1], oy1.at[1], p.to_yp),
            ]
        if r == 1:
            recv(*d_y1)
            sd_[p.ym, 0:32] = low_add(sd_[p.ym, 0:32], dy1[0]).astype(low)
            sd_[p.yp, 32:64] = low_add(sd_[p.yp, 32:64], dy1[1]).astype(low)
            d_y2 = [
                wire.send(sd_.at[p.ym], dy2.at[0], p.to_ym),
                wire.send(sd_.at[p.yp], dy2.at[1], p.to_yp),
            ]
            recv(*o_y1)
            ho[p.ym, 0] = low_add(ho[p.ym, 0], oy1[0]).astype(low)
            ho[p.yp, 1] = low_add(ho[p.yp, 1], oy1[1]).astype(low)
            o_y2 = [
                wire.send(ho.at[p.ym], oy2.at[0], p.to_ym),
                wire.send(ho.at[p.yp], oy2.at[1], p.to_yp),
            ]

        if r == 1:
            recv(*u_x2)
            lax.fori_loop(0, 8, add_us, 0)
            u_y1 = [
                wire.send(su_.at[p.y2, 0], uy1.at[0], p.to_ym),
                wire.send(su_.at[p.y2, 1], uy1.at[1], p.to_yp),
            ]

    dq_c = wire.send(dq_x.at[2], dq_x.at[c], p.sib)
    recv(*u_y1)
    su_[p.ym, 0] = low_add(su_[p.ym, 0], uy1[0]).astype(low)
    su_[p.yp, 1] = low_add(su_[p.yp, 1], uy1[1]).astype(low)
    u_y2 = [
        wire.send(su_.at[p.ym], uy2.at[0], p.to_ym),
        wire.send(su_.at[p.yp], uy2.at[1], p.to_yp),
    ]
    recv(*d_y2)
    dxx[x] = low_add(sd_[y], dy2[0], dy2[1]).astype(low)
    d_x = [wire.same(dxx.at[x], to_) for to_ in (p.to_xp, p.to_xm, p.to_x2)]
    recv(*o_y2)
    for k in range(2):
        to[k] = low_add(ho[y, k], oy2[0, k], oy2[1, k]).astype(low)
    o_z = [
        wire.send(to.at[zh, rows(32 * lo, 32)], oz1.at[0], p.to_zf),
        wire.send(to.at[zo, rows(32 * lo, 32)], oz1.at[1], p.to_zq),
        wire.send(to.at[zo, rows(32 * zl, 32)], oz1.at[2], p.to_z2),
    ]
    recv(nin_c)
    fft[...] = nin[...].reshape(768, D).T
    recv(dq_c)
    hq[...] = dot(fft[...], dq_x[0:2].reshape(768, 512)).astype(low).reshape(4, 2, 80, 512)

    def y_first(sums, landing):
        return [
            wire.send(sums.at[p.y2, 0], landing.at[0], p.to_ym),
            wire.send(sums.at[p.y2, 1], landing.at[1], p.to_yp),
        ]

    def y_second(sums, landed, landing):
        sums[p.ym, 0] = low_add(sums[p.ym, 0], landed[0]).astype(low)
        sums[p.yp, 1] = low_add(sums[p.yp, 1], landed[1]).astype(low)
        return [
            wire.send(sums.at[p.ym], landing.at[0], p.to_ym),
            wire.send(sums.at[p.yp], landing.at[1], p.to_yp),
        ]

    def z_all(total, sums, landed, landing):
        width = landing.shape[-1]
        for k in range(2):
            total[k] = low_add(sums[y, k], landed[0, k], landed[1, k]).astype(low)
        return [
            wire.send(total.at[zh, :, cols(width * lo, width)], landing.at[0], p.to_zf),
            wire.send(total.at[zo, :, cols(width * lo, width)], landing.at[1], p.to_zq),
            wire.send(total.at[zo, :, cols(width * zl, width)], landing.at[2], p.to_z2),
        ]

    def x_all(parts, total, landed):
        width = landed.shape[-1]
        mine = total[zh, :, cols(width * zl, width)]
        parts[x] = low_add(mine, landed[0], landed[1], landed[2]).astype(low)
        return [wire.same(parts.at[x], to_) for to_ in (p.to_xp, p.to_xm, p.to_x2)]

    def to_readers(result, parts):
        width = parts.shape[-1]
        mine = cols(2 * width * c + width * zl, width)
        result[:, mine] = low_add(parts[0], parts[1], parts[2], parts[3]).astype(low)
        return [wire.same(result.at[:, mine], to_) for to_ in (p.to_zf, p.sib, p.sib_zf)]

    q_y1 = y_first(hq, qy1)
    recv(*u_y2)
    for k in range(2):
        tu[k] = low_add(su_[y, k], uy2[0, k], uy2[1, k]).astype(low)
    u_z = [
        wire.send(tu.at[zh, :, cols(256 * lo, 256)], uz1.at[0], p.to_zf),
        wire.send(tu.at[zo, :, cols(256 * lo, 256)], uz1.at[1], p.to_zq),
        wire.send(tu.at[zo, :, cols(256 * zl, 256)], uz1.at[2], p.to_z2),
    ]

    recv(*kv_b)
    d_key = d_kv[512:896] + kv_in1[...].astype(f32)
    tail = jnp.concatenate([jnp.zeros((256, 512), f32), kv_in2[...].astype(f32)], axis=0)
    d_key = d_key + tail
    dk_x[slot_two] = d_key[:, HD:].astype(low)
    piece = turn_back(d_key[:, :HD], cos_ref[...], sin_ref[...])
    d_head, dg_key = norm_back(
        piece, proj[:, 1024 : 1024 + HD], qkv_scale[:, 4:5], gain_row(22, 2)
    )
    put_gain(22, dg_key)
    dk_x[slot_one] = d_head.astype(low)
    dk_c = wire.send(dk_x.at[2], dk_x.at[c], p.sib)

    recv(*q_y1)
    q_y2 = y_second(hq, qy1, qy2)
    recv(dk_c)
    hk[...] = dot(fft[...], dk_x[0:2].reshape(768, 256)).astype(low).reshape(4, 2, 80, 256)
    k_y1 = y_first(hk, ky1)

    d_normed = dot_nt(dq_x[slot_one], q_all[:, :, :, :512].reshape(D, 512)) + dot_nt(
        dq_x[slot_two], q_all[:, :, :, 512:].reshape(D, 512)
    )
    d_normed = d_normed + dot_nt(dk_x[slot_one], k_all[:, :, :, :256].reshape(D, 256))
    d_normed = d_normed + dot_nt(dk_x[slot_two], k_all[:, :, :, 256:].reshape(D, 256))
    recv(*k_y1)
    k_y2 = y_second(hk, ky1, ky2)
    inputs = tok_ref[...].astype(f32)
    d_input, dg_in = norm_back(d_normed, inputs, scale_of(inputs), gain_row(0, 5))
    dx_ref[...] += d_input

    put_gain(0, dg_in)
    put_gain(20, gc_query[...])
    g_c = wire.send(gc.at[1], gc.at[0], p.sib)

    recv(*q_y2)
    q_z = z_all(tq, hq, qy2, qz1)
    recv(g_c)
    gz[z] = gc[0] + gc[1]
    g_z = [wire.same(gz.at[z], to_) for to_ in (p.to_zf, p.to_zq, p.to_z2)]
    recv(*o_z)
    ox[x] = low_add(to[zh, rows(32 * zl, 32)], oz1[0], oz1[1], oz1[2]).astype(low)
    o_x = [wire.same(ox.at[x], to_) for to_ in (p.to_xp, p.to_xm, p.to_x2)]
    recv(*d_x)
    rd[zl] = low_add(dxx[0], dxx[1], dxx[2], dxx[3]).astype(low)
    d_f = wire.same(rd.at[zl], p.to_zf)
    recv(*u_z)
    ru[c, zl, x] = low_add(tu[zh, :, cols(256 * zl, 256)], uz1[0], uz1[1], uz1[2]).astype(low)
    u_a = [wire.same(ru.at[c, zl, x], to_) for to_ in (p.to_xp, p.to_xm, p.to_x2)]
    recv(*g_z)
    gy[y] = (gz[0] + gz[1]) + (gz[2] + gz[3])
    g_y = [wire.same(gy.at[y], to_) for to_ in (p.to_yp, p.to_ym, p.to_y2)]
    recv(*k_y2)
    k_z = z_all(tk, hk, ky2, kz1)
    recv(*q_z)
    q_x = x_all(qx, tq, qz1)
    recv(*o_x)
    ro[zl] = low_add(ox[0], ox[1], ox[2], ox[3]).astype(low)
    o_f = wire.same(ro.at[zl], p.to_zf)
    recv(*u_a)
    u_b = [wire.same(ru.at[c, zl], to_) for to_ in (p.to_zf, p.sib, p.sib_zf)]
    recv(*g_y)
    gx[x] = (gy[0] + gy[1]) + (gy[2] + gy[3])
    g_x = [wire.same(gx.at[x], to_) for to_ in (p.to_xp, p.to_xm, p.to_x2)]
    recv(*k_z)
    k_x = x_all(kx, tk, kz1)
    recv(*q_x)
    q_f = to_readers(rq, qx)
    recv(*g_x)
    tg[...] = (gx[0] + gx[1]) + (gx[2] + gx[3])
    recv(*k_x)
    k_f = to_readers(rk, kx)
    recv(d_f, o_f, *u_b, *q_f, *k_f)
    wire.drain()


def layer(tokens, cotangent, places, weights, gains):
    low, f32 = jnp.bfloat16, jnp.float32
    owner = lax.axis_index("batch") * 4 + lax.axis_index("shard")
    own_gains = lax.dynamic_update_slice(
        jnp.zeros((3072,), f32), gains.astype(low).astype(f32), (owner * 192,)
    ).reshape(24, 128)

    def vm(*shape, kind=low):
        return pltpu.VMEM(shape, kind)

    spaces = [pl.ANY] * 2 + [pltpu.VMEM] * 2 + [pl.ANY] * 4 + [pltpu.VMEM]
    outs = [
        ((384, D), low), ((384, D), f32), ((80, 1024), low), ((80, 512), low), ((2, 32, D), low),
        ((2, 2, 4, 80, 256), low), ((2, 64, D), low), ((24, 128), f32),
    ]
    return pl.pallas_call(
        layer_kernel,
        out_shape=[jax.ShapeDtypeStruct(s, k) for s, k in outs],
        in_specs=[pl.BlockSpec(memory_space=space) for space in spaces],
        out_specs=[pl.BlockSpec(memory_space=pltpu.VMEM)] * 8,
        scratch_shapes=[
            vm(384, D), vm(384, D), vm(384, 128, kind=f32), vm(384, 128, kind=f32),
            vm(384, 128, kind=f32), vm(40, 256, kind=f32), vm(40, 512, kind=f32),
            vm(40, 512, kind=f32), vm(64, D, kind=f32), vm(128, D, kind=f32), pltpu.SemaphoreType.DMA((7,)),
            vm(4, 2, 80, 1024), vm(4, 2, 80, 512), vm(4, 2, 2, 64, D), vm(4, 2, 80, 4096), vm(4, 2, 2, 128, D),
            vm(40, 512, kind=f32), vm(40, 256, kind=f32), vm(40, 512, kind=f32),
            vm(2, 24, 128, kind=f32), vm(2, 24, 128, kind=f32), vm(4, 24, 128, kind=f32),
            vm(24, 128, kind=f32),
            vm(2, 384, D), vm(384, 1280, kind=f32), vm(384, 128, kind=f32), vm(4, 384, HD),
            vm(896, 512), vm(3, 512, 640), vm(384, 1024), vm(384, D, kind=f32),
            vm(384, D, kind=f32), vm(2, 384, D), vm(3, 384, 1536),
            vm(8, 3, 384, 128), vm(1, HD, kind=f32),
            vm(2, 384, D), vm(3, 384, FF), vm(384, 1024),
            vm(896, 512, kind=f32), vm(512, 512), vm(384, 512), vm(128, 512),
            vm(D, 768),
            vm(4, 2, 2, 64, D), vm(4, 2, 64, D),
            vm(D, 2048), vm(4, 2, 80, 512), vm(4, 2, 80, 256), vm(4, 2, 64, D), vm(4, 2, 2, 64, D),
            vm(2, D, 256), vm(2, D, 512), vm(4, 2, 80, 512),
            vm(2, 80, 512), vm(2, 2, 80, 512), vm(2, 80, 512),
            vm(3, 80, 256),
            vm(2, 80, 512), vm(2, 2, 80, 512), vm(2, 80, 512), vm(3, 80, 256), vm(4, 80, 256),
            vm(2, 80, 256), vm(2, 2, 80, 256), vm(2, 80, 256), vm(3, 80, 128), vm(4, 80, 128),
            vm(2, 64, D), vm(2, 2, 64, D), vm(2, 64, D),
            vm(3, 32, D), vm(4, 32, D),
            vm(2, 2, 64, D), vm(2, 4, 64, D), vm(4, 64, D),
            vm(2, 32, D), vm(2, 64, D), vm(4, 64, D),
            vm(2, 24, 128, kind=f32), vm(4, 24, 128, kind=f32),
            vm(4, 24, 128, kind=f32), vm(4, 24, 128, kind=f32),
            pltpu.SemaphoreType.DMA((COPIES,)),
            pltpu.SemaphoreType.DMA((COPIES,)),
        ],
        compiler_params=pltpu.CompilerParams(
            collective_id=0, has_side_effects=True, vmem_limit_bytes=62 * 1024 * 1024
        ),
        name="layer",
    )(tokens, cotangent, places, tables(), *weights, own_gains)


SHAPES = [(40, 1536), (64, D), (40, 4096), (128, D)]


def adam_kernel(*refs):
    dx_hbm, y_hbm, rk_hbm = refs[:3]
    ins, (dx_out, y_out), outs = refs[3:19], refs[19:21], refs[21:33]
    held, made, (dx_vm, y_vm, rk_vm) = refs[33:49], refs[49:61], refs[61:64]
    in_sems, out_sems, pass_sems = refs[64:]
    c = lax.rem(lax.axis_index("shard"), 2)
    order = (0, 1, 3, 2)
    fetches, stores = {}, []
    for k in order:
        for n in range(4 * k, 4 * k + 4):
            fetches[n] = pltpu.make_async_copy(ins[n], held[n], in_sems.at[n])
            fetches[n].start()
    rest = [
        pltpu.make_async_copy(src, dst, pass_sems.at[n])
        for n, (src, dst) in enumerate(((rk_hbm, rk_vm), (dx_hbm, dx_vm), (y_hbm, y_vm)))
    ]
    for copy in rest:
        copy.start()

    def own_rows(total):
        total = total.astype(jnp.float32)
        return jnp.where(c == 0, total[:40], total[40:])

    for k in order:
        for n in range(4 * k, 4 * k + 4):
            fetches[n].wait()
        total, weight, one, two = held[4 * k : 4 * k + 4]
        new, mean, square = made[3 * k : 3 * k + 3]

        def adam_into(part, gradient):
            new[part], mean[part], square[part] = adamw(
                weight[part], gradient, one[part], two[part], WEIGHT_DECAY
            )

        if k == 0:
            rest[0].wait()
            adam_into((slice(None), slice(0, 1024)), own_rows(total[...]))
            adam_into((slice(None), slice(1024, 1536)), own_rows(rk_vm[...]))
        elif k == 2:
            for core in range(2):
                for ax in range(4):
                    for zl in range(2):
                        start = 2048 * core + 512 * ax + 256 * zl
                        adam_into(
                            (slice(None), slice(start, start + 256)),
                            own_rows(total[core, zl, ax]),
                        )
        else:
            height = total.shape[1]
            for n in range(2):
                adam_into(slice(height * n, height * (n + 1)), total[n].astype(jnp.float32))
        for n in range(3 * k, 3 * k + 3):
            stores.append(pltpu.make_async_copy(made[n], outs[n], out_sems.at[n]))
            stores[-1].start()
        if k == 3:
            for n, (src, dst) in enumerate(((dx_vm, dx_out), (y_vm, y_out))):
                rest[1 + n].wait()
                stores.append(pltpu.make_async_copy(src, dst, pass_sems.at[3 + n]))
                stores[-1].start()
    for copy in stores:
        copy.wait()


def update(dx, y, rk, totals, weights, firsts, seconds):
    f32 = jnp.float32
    ins = [a for k in range(4) for a in (totals[k], weights[k], firsts[k], seconds[k])]
    results = [jax.ShapeDtypeStruct(s, f32) for s in SHAPES for _ in range(3)]
    dx, y, *made = pl.pallas_call(
        adam_kernel,
        out_shape=[jax.ShapeDtypeStruct(a.shape, a.dtype) for a in (dx, y)] + results,
        in_specs=[pl.BlockSpec(memory_space=pl.ANY)] * 19,
        out_specs=[pl.BlockSpec(memory_space=pl.ANY)] * 14,
        scratch_shapes=[pltpu.VMEM(a.shape, a.dtype) for a in ins]
        + [pltpu.VMEM(a.shape, a.dtype) for a in results]
        + [pltpu.VMEM(a.shape, a.dtype) for a in (dx, y, rk)]
        + [pltpu.SemaphoreType.DMA((n,)) for n in (16, 12, 5)],
        compiler_params=pltpu.CompilerParams(vmem_limit_bytes=62 * 1024 * 1024),
        name="update",
    )(dx, y, rk, *ins)
    return (dx, y, *made[0::3], *made[1::3], *made[2::3])


def shards(
    tokens, cotangent, positions,
    weight_qkv, weight_out, weight_up, weight_down, norm_gains,
    first_qkv, first_out, first_up, first_down, first_gains,
    second_qkv, second_out, second_up, second_down, second_gains,
):
    weights = (weight_qkv, weight_out, weight_up, weight_down)
    y, dx, rq, rk, ro, ru, rd, tg = layer(
        tokens[0], cotangent[0], positions[0].reshape(3, 128), weights, norm_gains
    )
    dx, y, *results = update(
        dx, y, rk, (rq, ro, ru, rd), weights,
        (first_qkv, first_out, first_up, first_down),
        (second_qkv, second_out, second_up, second_down),
    )
    owner = lax.axis_index("batch") * 4 + lax.axis_index("shard")
    total_gains = lax.dynamic_slice_in_dim(tg.reshape(3072), owner * 192, 192)
    new_gains, mean_gains, square_gains = adamw(
        norm_gains, total_gains, first_gains, second_gains, 0.0
    )
    return (
        y[None], dx[None],
        *results[0:4], new_gains, *results[4:8], mean_gains, *results[8:12], square_gains,
    )


def solution(mesh):
    return jax.shard_map(
        shards,
        mesh=mesh,
        in_specs=(
            P(("batch", "shard"), "seq", None),
            P(("batch", "shard"), "seq", None),
            P(("batch", "shard"), "seq"),
            P(("batch", "shard"), None),
            P(("batch", "shard"), None),
            P(("batch", "shard"), None),
            P(("batch", "shard"), None),
            P(("batch", "shard")),
            P(("batch", "shard"), None),
            P(("batch", "shard"), None),
            P(("batch", "shard"), None),
            P(("batch", "shard"), None),
            P(("batch", "shard")),
            P(("batch", "shard"), None),
            P(("batch", "shard"), None),
            P(("batch", "shard"), None),
            P(("batch", "shard"), None),
            P(("batch", "shard")),
        ),
        out_specs=(
            P(("batch", "shard"), "seq", None),
            P(("batch", "shard"), "seq", None),
            P(("batch", "shard"), None),
            P(("batch", "shard"), None),
            P(("batch", "shard"), None),
            P(("batch", "shard"), None),
            P(("batch", "shard")),
            P(("batch", "shard"), None),
            P(("batch", "shard"), None),
            P(("batch", "shard"), None),
            P(("batch", "shard"), None),
            P(("batch", "shard")),
            P(("batch", "shard"), None),
            P(("batch", "shard"), None),
            P(("batch", "shard"), None),
            P(("batch", "shard"), None),
            P(("batch", "shard")),
        ),
        check_vma=False,
    )
```

time: 743 us -> 156 us (0.21)
  waiting for transfers between devices: 446 us -> 0 us
  Pallas kernels: 0 us -> 149 us
  blocking collectives: 124 us -> 0 us
  matrix products: 63.8 us -> 0 us
  other arithmetic: 45.1 us -> 2.04 us
  local copies, waits for them, and re-layouts: 26 us -> 2.62 us
  between operations: 17 us -> 0.9 us
  starting transfers between devices: 12.1 us -> 0 us
    reduce_scatter x4 -> x0, waiting for transfers between devices: 287 us -> none  [the longest x1 116 us: shards(): lax.psum_scatter(grad_up, ('batch', 'shard'), scatter_dimension=0, tiled=...]
    pallas_call x0 -> x2, Pallas kernels: none -> 149 us  [the longest x1 144 us: layer(): pl.pallas_call(layer_kernel, out_shape=[jax.ShapeDtypeStruct(s, k) for s,...]
    all_gather x4 -> x0, waiting for transfers between devices: 112 us -> none  [the longest x1 56.5 us: shards(): lax.all_gather(weight_up.astype(jnp.bfloat16), ('batch', 'shard'), axis=0...]
    unnamed x2 -> x0, blocking collectives: 105 us -> none
    dot_general x18 -> x0, matrix products: 63.8 us -> none  [the longest x1 9.89 us: shards(): jnp.einsum('td,tf->df', ff_low, d_gate_low, preferred_element_type=jnp.fl...]
    ppermute x4 -> x0, waiting for transfers between devices: 46.7 us -> none  [passed_along(): return lax.ppermute(block, axis, route)]
    psum x1 -> x0, blocking collectives: 19.4 us -> none  [shards(): lax.psum((owned_qkv, owned_out, owned_up, owned_down, owned_gains), 'seq')]
    unnamed x203 -> x10, local copies, waits for them, and re-layouts: 19 us -> 2.62 us
  transfers between devices with their start and end apart: 13 -> 0, of which waited for: 12 -> 0; matrix products, arithmetic and copies ran while one was open for 13% -> 0% of each run, Pallas kernels for 0% -> 0%
where the time goes in v1:
time: 156 us; the launch traced here: 155 us
  Pallas kernels  149 us (96%)
  local copies, waits for them, and re-layouts  2.62 us (2%)
  other arithmetic  2.04 us (1%)
    pallas_call x1, Pallas kernels, layer(): pl.pallas_call(layer_kernel, out_shape=[jax.ShapeDtypeStruct(s, k) for s,...  144 us
    pallas_call x1, Pallas kernels, update(): pl.pallas_call(adam_kernel, out_shape=[jax.ShapeDtypeStruct(a.shape, a.dt...  5.19 us

profile of v1, /device:TPU:0, one launch (start us, length us, event | category | flops | bytes accessed | tf_op | source)
XLA Modules:
  0.0 154.5 jit_solution(1997004540816445927)
XLA Ops:
  0.7 0.0 copy-start.2
  0.7 0.7 copy-done.2
  1.3 0.6 reduce
  1.9 0.0 copy-start.1
  1.9 0.7 copy-done.1
  2.6 0.1 convert_dynamic-update-slice_fusion
  2.7 0.0 copy-start
  2.7 0.6 copy-done
  3.3 0.0 copy-start.4
  3.3 143.8 %layer.1 = (bf16[384,640]{1,0:T(8,128)(2,1)}, f32[384,640]{1,0:T(8,128)}, bf16[80,1024]{1,0:T(8,128)(2,1)}, bf16[80,512]{1,0:T(8,128)(2,1)}, bf16[2,32,640]{2,1,...) custom-call(bf16[384,640]{1,0:T(8,128)(2,1)} %bitcast.7, ...), custom_call_target="tpu_custom_call" | custom-call | tf_op jit(solution)/shard_map/layer/pallas_call | solution.py:776
  147.1 0.0 copy-start.3
  147.1 0.0 copy-done.4
  147.1 0.7 copy-done.3
  147.8 1.4 multiply_subtract_fusion
  149.1 5.2 %update.1 = (f32[384,640]{1,0:T(8,128)}, bf16[384,640]{1,0:T(8,128)(2,1)}, f32[40,1536]{1,0:T(8,128)}, f32[40,1536]{1,0:T(8,128)}, f32[40,1536]{1,0:T(8,128)}, /...) custom-call(f32[384,640]{1,0:T(8,128)} %get-tuple-element.39.refs_0_, ...), custom_call_target="tpu_custom_call" | custom-call | tf_op jit(solution)/shard_map/update/pallas_call | solution.py:889
  (1 shorter events, 0.0 us)
Async XLA Ops:
  0.7 0.7 copy-start.2
  1.9 0.7 copy-start.1
  2.7 0.6 copy-start
  3.3 143.8 %copy-start.4 = (f32[192]{0:T(256)S(1)}, f32[192]{0:T(256)}, u32[]{:S(2)}) copy-start(f32[192]{0:T(256)} %param.36) | copy-start | bytes 2308
  147.1 0.7 copy-start.3
